TPU v7x, 512 devices: a whole 4x4x16 slice. The times are simulated.
512 devices in a mesh: row: 16 (over x, y), col: 32 (over z, core).
Axes of the slice: x: 4, y: 4, z: 16, core: 2. Of those that a mesh axis runs over, the one named last changes fastest.
Arguments:
- species: float32 [512, 256, 2048], P(None, 'col', 'row'), may hold values from -26 to 26, as said below
- start_basis: float32 [512, 256], replicated, may hold values from -6 to 6
Outputs:
- core_fibers: float32 [256, 256, 2048], P('row', 'col')
- basis: float32 [512, 256], replicated
Inputs may be any that keep to these rules, and one draw needn't show every extreme that they name: `species`: entries of the slab.
All inputs are finite; a program needn't handle non-finite values.
Results may differ from a plain program's by a relative error of at most 0.00019.
Values sent between devices are 32-bit elements; how exact they have to be, the bound alone decides.
No kernel may reach another device: no remote copies, remote signals or barrier semaphores. Data moves between devices by JAX's collectives and lax.ppermute only.
A program may use at most 64 MiB of HBM per device.

v0:
```python
import jax
import jax.numpy as jnp
from jax import lax
from jax.sharding import PartitionSpec as P

ITERS = 2


def orthonormalize(applied):
    inner_gram = jnp.dot(
        applied.T, applied, precision=lax.Precision.HIGHEST, preferred_element_type=jnp.float32
    )
    small_lower = jnp.linalg.cholesky(inner_gram)
    return jax.scipy.linalg.solve_triangular(small_lower, applied.T, lower=True).T


def power_steps(tri_lower, start_basis):
    current = start_basis
    for sweep_number in range(ITERS):
        halfway = jnp.dot(
            tri_lower.T,
            current,
            precision=lax.Precision.HIGHEST,
            preferred_element_type=jnp.float32,
        )
        applied = jnp.dot(
            tri_lower, halfway, precision=lax.Precision.HIGHEST, preferred_element_type=jnp.float32
        )
        current = orthonormalize(applied)
    return current


def shards(species, start_basis):
    width_x, cells_z, cells_y = species.shape
    fibers = species.reshape(width_x, cells_z * cells_y)
    local_gram = jnp.dot(
        fibers, fibers.T, precision=lax.Precision.HIGHEST, preferred_element_type=jnp.float32
    )
    gram_sum = lax.psum(local_gram, ("row", "col"))
    basis = power_steps(jnp.linalg.cholesky(gram_sum), start_basis)
    core_flat = jnp.dot(
        basis.T, fibers, precision=lax.Precision.HIGHEST, preferred_element_type=jnp.float32
    )
    core_block = core_flat.reshape(basis.shape[1], cells_z, cells_y)
    core_fibers = lax.all_to_all(core_block, "row", split_axis=0, concat_axis=2, tiled=True)
    return (core_fibers, basis)


def solution(mesh):
    in_specs = (P(None, "col", "row"), P())
    out_specs = (P("row", "col", None), P())
    return jax.shard_map(shards, mesh=mesh, in_specs=in_specs, out_specs=out_specs, check_vma=False)
```

profile of v0, /device:TPU:1, one launch (start us, length us, event | category | flops | bytes accessed | tf_op | source)
XLA Modules:
  0.0 744.2 jit_solution(14799633142379794219)
XLA Ops:
  7.2 7.1 fusion.2
  14.4 2.1 copy.41
  16.4 2.0 copy.25
  18.5 468.3 %all-reduce.4.cloned.1.call-done = f32[512,512]{0,1:T(8,128)} async-done(((f32[512,512]{0,1:T(8,128)}), f32[512,512]{0,1:T(8,128)}) %all-reduce.4.cloned.1.call-update) | async-done | bytes 1048592 | tf_op jit(solution)/shard_map/psum | solution.py:39
  486.7 1.6 copy.19
  489.6 11.7 %cholesky.136 = f32[128,128]{1,0:T(8,128)S(1)} custom-call(f32[128,128]{1,0:T(8,128)S(1)} %cholesky.407), custom_call_target="Cholesky" | custom-call | tf_op jit(solution)/shard_map/jit(cholesky)/cholesky | solution.py:40
  501.3 9.8 %custom-call.32 = f32[1,128,128]{1,2,0:T(8,128)S(1)} custom-call(f32[1,128,128]{2,1,0:T(8,128)S(1)} %get-tuple-element.62), custom_call_target="InvertDiagBlocksLowerTriangular" | custom-call | tf_op jit(solution)/shard_map/jit(cholesky)/cholesky | solution.py:40
  513.8 11.7 %cholesky.159 = f32[128,128]{1,0:T(8,128)S(1)} custom-call(f32[128,128]{1,0:T(8,128)S(1)} %cholesky.411), custom_call_target="Cholesky" | custom-call | tf_op jit(solution)/shard_map/jit(cholesky)/cholesky | solution.py:40
  525.6 10.0 %custom-call.33 = f32[1,128,128]{1,2,0:T(8,128)S(1)} custom-call(f32[1,128,128]{2,1,0:T(8,128)S(1)} %get-tuple-element.59), custom_call_target="InvertDiagBlocksLowerTriangular" | custom-call | tf_op jit(solution)/shard_map/jit(cholesky)/cholesky | solution.py:40
  535.8 1.3 convolution_subtract_fusion.3
  537.1 11.7 %cholesky.294 = f32[128,128]{1,0:T(8,128)S(1)} custom-call(f32[128,128]{1,0:T(8,128)S(1)} %cholesky.416), custom_call_target="Cholesky" | custom-call | tf_op jit(solution)/shard_map/jit(cholesky)/cholesky | solution.py:40
  549.5 9.8 %custom-call.39 = f32[1,128,128]{1,2,0:T(8,128)S(1)} custom-call(f32[1,128,128]{2,1,0:T(8,128)S(1)} %get-tuple-element.56), custom_call_target="InvertDiagBlocksLowerTriangular" | custom-call | tf_op jit(solution)/shard_map/jit(cholesky)/cholesky/custom-call.9 | solution.py:40
  560.8 11.7 %cholesky.307 = f32[128,128]{1,0:T(8,128)S(1)} custom-call(f32[128,128]{1,0:T(8,128)S(1)} %convolution_subtract_fusion.6), custom_call_target="Cholesky" | custom-call | tf_op jit(solution)/shard_map/jit(cholesky)/cholesky | solution.py:40
  576.4 1.7 fusion.15
  580.3 11.7 %cholesky.357 = f32[128,128]{1,0:T(8,128)S(1)} custom-call(f32[128,128]{1,0:T(8,128)S(1)} %cholesky.420), custom_call_target="Cholesky" | custom-call | tf_op jit(solution)/shard_map/jit(cholesky)/cholesky | solution.py:13
  592.7 9.8 %custom-call.40 = f32[1,128,128]{1,2,0:T(8,128)S(1)} custom-call(f32[1,128,128]{2,1,0:T(8,128)S(1)} %get-tuple-element.52), custom_call_target="InvertDiagBlocksLowerTriangular" | custom-call | tf_op jit(solution)/shard_map/jit(cholesky)/cholesky/custom-call.9 | solution.py:13
  603.0 11.8 %cholesky.367 = f32[128,128]{1,0:T(8,128)S(1)} custom-call(f32[128,128]{1,0:T(8,128)S(1)} %convolution_subtract_fusion.5), custom_call_target="Cholesky" | custom-call | tf_op jit(solution)/shard_map/jit(cholesky)/cholesky | solution.py:13
  616.9 4.0 while.4
  617.5 1.4 bitcast_dynamic-update-slice_fusion.4
  619.6 1.4 bitcast_dynamic-update-slice_fusion.4
  620.9 19.7 %custom-call.41 = f32[2,128,128]{1,2,0:T(8,128)S(1)} custom-call(f32[2,128,128]{2,1,0:T(8,128)S(1)} %get-tuple-element.19), custom_call_target="InvertDiagBlocksLowerTriangular" | custom-call | tf_op jit(solution)/shard_map/jit(_solve_triangular)/triangular_solve | solution.py:14
  645.5 11.7 %cholesky.384 = f32[128,128]{1,0:T(8,128)S(1)} custom-call(f32[128,128]{1,0:T(8,128)S(1)} %cholesky.423), custom_call_target="Cholesky" | custom-call | tf_op jit(solution)/shard_map/jit(cholesky)/cholesky | solution.py:13
  657.9 9.8 %custom-call.42 = f32[1,128,128]{1,2,0:T(8,128)S(1)} custom-call(f32[1,128,128]{2,1,0:T(8,128)S(1)} %get-tuple-element.48), custom_call_target="InvertDiagBlocksLowerTriangular" | custom-call | tf_op jit(solution)/shard_map/jit(cholesky)/cholesky/custom-call.9 | solution.py:13
  668.2 11.9 %cholesky.394 = f32[128,128]{1,0:T(8,128)S(1)} custom-call(f32[128,128]{1,0:T(8,128)S(1)} %convolution_subtract_fusion.4), custom_call_target="Cholesky" | custom-call | tf_op jit(solution)/shard_map/jit(cholesky)/cholesky | solution.py:13
  682.2 4.0 while.5
  682.8 1.4 bitcast_dynamic-update-slice_fusion.5
  684.8 1.4 bitcast_dynamic-update-slice_fusion.5
  686.2 19.7 %custom-call.43 = f32[2,128,128]{1,2,0:T(8,128)S(1)} custom-call(f32[2,128,128]{2,1,0:T(8,128)S(1)} %get-tuple-element.20), custom_call_target="InvertDiagBlocksLowerTriangular" | custom-call | tf_op jit(solution)/shard_map/jit(_solve_triangular)/triangular_solve | solution.py:14
  707.3 3.5 fusion.11
  710.8 1.6 copy.26
  712.4 6.2 all-to-all-start
  719.7 16.4 %all-to-all-done = f32[256,8,128]{2,1,0:T(8,128)S(1)} async-done(((f32[256,8,128]{2,1,0:T(8,128)}), f32[256,8,128]{2,1,0:T(8,128)S(1)}, u32[]{:S(2)}, u32[]{:S(2)}) %all-to-all-start) | async-done | bytes 1048608 | tf_op jit(solution)/shard_map/all_to_all | solution.py:45
  (73 shorter events, 24.4 us)
Async XLA Ops:
  7.2 569.2 %copy-start = (f32[512,256]{1,0:T(8,128)S(1)}, f32[512,256]{1,0:T(8,128)}, u32[]{:S(2)}) copy-start(f32[512,256]{1,0:T(8,128)} %param.8) | copy-start | bytes 1572868
  7.2 479.5 %all-reduce.4.cloned.1.call-start = ((), (), s32[]{:S(2)}) async-start(), calls=%async_computation.1 | async-start | bytes 2097152 | tf_op jit(solution)/shard_map/psum | solution.py:39
  486.7 1.7 copy-start.1
  488.6 1.0 copy-start.2
  712.4 23.6 %all-to-all-start = ((f32[256,8,128]{2,1,0:T(8,128)}), f32[256,8,128]{2,1,0:T(8,128)S(1)}, u32[]{:S(2)}, u32[]{:S(2)}) async-start(f32[256,8,128]{2,1,0:T(8,128)} %copy.26), calls=%async_computation | async-start | bytes 2097152 | tf_op jit(solution)/shard_map/all_to_all | solution.py:45
Sparse Core Ops, SparseCore 0:
  14.5 472.1 all-reduce.3
where the time goes:
time: 749 us; the launch traced here: 744 us
  waiting for transfers between devices  485 us (65%)
  other arithmetic  188 us (25%)
  matrix products  26.8 us (4%)
  between operations  19.8 us (3%)
  local copies, waits for them, and re-layouts  18.8 us (3%)
    psum x1, waiting for transfers between devices, shards(): gram_sum = lax.psum(local_gram, ('row', 'col'))  468 us
    another operation x14, other arithmetic, shards(): basis = power_steps(jnp.linalg.cholesky(gram_sum), start_basis)  78.6 us
    another operation x14, other arithmetic, orthonormalize(): small_lower = jnp.linalg.cholesky(inner_gram)  69.5 us
    another operation x5, other arithmetic, orthonormalize(): jax.scipy.linalg.solve_triangular(small_lower, applied.T, lower=True)  39.4 us
    all_to_all x1, waiting for transfers between devices, shards(): lax.all_to_all(core_block, 'row', split_axis=0, concat_axis=2, tiled=True)  16.4 us
  transfers between devices with their start and end apart: 2, of which 2 were waited for; matrix products, arithmetic and copies ran while one was open for 1% of the time, Pallas kernels for 0%

commit v1 on v0

v1 whole, which is shorter than its diff:
```python
import jax
import jax.numpy as jnp
from jax import lax
from jax.experimental import pallas as pl
from jax.experimental.pallas import tpu as pltpu
from jax.sharding import Mesh, PartitionSpec as P

ITERS = 2
TILE = 128
PANEL = 8
NT = (((1,), (1,)), ((), ()))
NN = (((1,), (0,)), ((), ()))
PARAMS = pltpu.CompilerParams(vmem_limit_bytes=40 * 2**20)


def matmul(left, right, dims=NN):
    return lax.dot_general(
        left, right, dims, precision=lax.Precision.HIGHEST, preferred_element_type=jnp.float32
    )


def halves(value):
    high = value.astype(jnp.bfloat16)
    return high, (value - high.astype(jnp.float32)).astype(jnp.bfloat16)


def dot16(left, right, dims):
    return lax.dot_general(left, right, dims, preferred_element_type=jnp.float32)


def lower_tiles(count):
    return [(i, j) for i in range(count) for j in range(i + 1)]


def gram_kernel(x_ref, packed_ref, high_ref, low_ref):
    width, cells_z, cells_y = x_ref.shape
    flat = x_ref.reshape(width * cells_z, cells_y)
    for z in range(cells_z):
        high, low = halves(flat[pl.ds(z, width, stride=cells_z), :])
        high_ref[:, z * cells_y : (z + 1) * cells_y] = high
        low_ref[:, z * cells_y : (z + 1) * cells_y] = low
    side = 2 * TILE
    for i, j in lower_tiles(width // side):
        rows, columns = pl.ds(i * side, side), pl.ds(j * side, side)
        block = dot16(high_ref[rows, :], high_ref[columns, :], NT)
        cross = dot16(high_ref[rows, :], low_ref[columns, :], NT)
        if i == j:
            block = block + (cross + cross.T)
        else:
            block = block + (cross + dot16(low_ref[rows, :], high_ref[columns, :], NT))
        for place, (a, b) in enumerate(lower_tiles(width // TILE)):
            if (a // 2, b // 2) == (i, j):
                ra, rb = (a % 2) * TILE, (b % 2) * TILE
                packed_ref[place * TILE : (place + 1) * TILE, :] = block[ra : ra + TILE, rb : rb + TILE]


def spread_row(tile, k):
    return jnp.broadcast_to(tile[k : k + 1, :], tile.shape)


def spread_column(tile, k):
    return jnp.broadcast_to(tile[:, k : k + 1], tile.shape)


def inverse_factor(matrix):
    size = matrix.shape[0]
    count = size // PANEL
    tiles = [matrix[PANEL * t : PANEL * (t + 1), :] for t in range(count)]
    sub = lax.broadcasted_iota(jnp.int32, (PANEL, size), 0)
    lane = lax.broadcasted_iota(jnp.int32, (PANEL, size), 1)
    done = []
    for t in range(count):
        first = PANEL * t
        panel = (lane >= first) & (lane < first + PANEL)
        columns = [spread_column(tiles[t], first + k) for k in range(PANEL)]
        rest = jnp.where(panel, jnp.where(lane - first == sub, 1.0, 0.0), tiles[t])
        forward, pivots = rest, columns[0]
        for k in range(PANEL):
            here = sub == k
            reciprocal = 1.0 / spread_row(columns[k], k)
            if k:
                forward = jnp.where(sub >= k, rest, forward)
                pivots = jnp.where(here, columns[k], pivots)
            for j in range(k + 1, PANEL):
                scaled = spread_row(columns[j], k) * reciprocal
                columns[j] = jnp.where(here, scaled, columns[j] - columns[k] * scaled)
            scaled = spread_row(rest, k) * reciprocal
            rest = jnp.where(here, scaled, rest - columns[k] * scaled)
        done.append(jnp.where(lane <= first + sub, forward * lax.rsqrt(pivots), 0.0))
        rows = [spread_row(rest, k) for k in range(PANEL)]
        for i in range(t + 1, count):
            total = jnp.where(panel, 0.0, tiles[i])
            for k in range(PANEL):
                total = total - spread_column(tiles[i], first + k) * rows[k]
            tiles[i] = total
    return jnp.concatenate(done, axis=0)


def orthonormal(applied_t):
    half = applied_t.shape[0] // 2
    inner = matmul(applied_t, applied_t, NT)
    inverse_a = inverse_factor(inner[:half, :half])
    below = matmul(inner[half:, :half], inverse_a, NT)
    inverse_b = inverse_factor(inner[half:, half:] - matmul(below, below, NT))
    first = matmul(inverse_a, applied_t[:half])
    second = matmul(inverse_b, applied_t[half:] - matmul(below, first))
    return jnp.concatenate([first, second], axis=0)


def basis_kernel(packed_ref, start_ref, high_ref, low_ref, core_ref, basis_ref, gram_ref):
    width = start_ref.shape[0]
    rank, cells_z, cells_y = core_ref.shape
    for place, (a, b) in enumerate(lower_tiles(width // TILE)):
        tile = packed_ref[place * TILE : (place + 1) * TILE, :]
        gram_ref[a * TILE : (a + 1) * TILE, b * TILE : (b + 1) * TILE] = tile
        if a != b:
            gram_ref[b * TILE : (b + 1) * TILE, a * TILE : (a + 1) * TILE] = tile.T
    current_t = start_ref[...].T
    for sweep_number in range(ITERS):
        current_t = orthonormal(matmul(current_t, gram_ref[...]))
    basis_ref[...] = current_t.T
    high, low = halves(current_t)
    flat = core_ref.reshape(rank * cells_z, cells_y)
    for z in range(0, cells_z, 2):
        columns = pl.ds(z * cells_y, 2 * cells_y)
        block = dot16(high, high_ref[:, columns], NN) + (
            dot16(high, low_ref[:, columns], NN) + dot16(low, high_ref[:, columns], NN)
        )
        flat[pl.ds(z, rank, stride=cells_z), :] = block[:, :cells_y]
        flat[pl.ds(z + 1, rank, stride=cells_z), :] = block[:, cells_y:]


def exchange(value, axes):
    return lax.all_to_all(value, axes, split_axis=0, concat_axis=0, tiled=True)


def sum_over(value, axes, members):
    return exchange(jnp.broadcast_to(value, (members, *value.shape)), axes).sum(axis=0)


def shards(species, start_basis):
    width, cells_z, cells_y = species.shape
    rank = start_basis.shape[1]
    tiles = len(lower_tiles(width // TILE))
    packed, high, low = pl.pallas_call(
        gram_kernel,
        out_shape=(
            jax.ShapeDtypeStruct((tiles * TILE, TILE), jnp.float32),
            jax.ShapeDtypeStruct((width, cells_z * cells_y), jnp.bfloat16),
            jax.ShapeDtypeStruct((width, cells_z * cells_y), jnp.bfloat16),
        ),
        compiler_params=PARAMS,
        name="gram",
    )(species)
    plane = ("row", "core")
    members = lax.axis_size(plane)
    part = exchange(packed.reshape(members, -1, TILE), plane).sum(axis=0)
    part = sum_over(part, "zl", lax.axis_size("zl"))
    part = sum_over(part, "zh", lax.axis_size("zh"))
    packed = exchange(jnp.broadcast_to(part, (members, *part.shape)), plane)
    core, basis = pl.pallas_call(
        basis_kernel,
        out_shape=(
            jax.ShapeDtypeStruct((rank, cells_z, cells_y), jnp.float32),
            jax.ShapeDtypeStruct((width, rank), jnp.float32),
        ),
        scratch_shapes=[pltpu.VMEM((width, width), jnp.float32)],
        compiler_params=PARAMS,
        name="basis",
    )(packed.reshape(-1, TILE), start_basis, high, low)
    core = lax.all_to_all(core, "row", split_axis=0, concat_axis=2, tiled=True)
    return core, basis


def solution(mesh):
    rows, columns = mesh.devices.shape
    fine = Mesh(mesh.devices.reshape(rows, columns // 8, 4, 2), ("row", "zh", "zl", "core"))
    split = ("zh", "zl", "core")
    return jax.shard_map(
        shards,
        mesh=fine,
        in_specs=(P(None, split, "row"), P()),
        out_specs=(P("row", split, None), P()),
        check_vma=False,
    )
```

time: 749 us -> 125 us (0.17)
  waiting for transfers between devices: 485 us -> 0 us
  other arithmetic: 188 us -> 0.07 us
  blocking collectives: 0 us -> 93.6 us
  Pallas kernels: 0 us -> 27.6 us
  matrix products: 26.8 us -> 0 us
  between operations: 19.8 us -> 0.68 us
  local copies, waits for them, and re-layouts: 18.8 us -> 2.73 us
    psum x1 -> x0, waiting for transfers between devices: 468 us -> none  [shards(): gram_sum = lax.psum(local_gram, ('row', 'col'))]
    another operation x33 -> x0, other arithmetic: 187 us -> none  [the longest x14 78.6 us: shards(): basis = power_steps(jnp.linalg.cholesky(gram_sum), start_basis)]
    all_to_all x0 -> x5, blocking collectives: none -> 93.6 us  [the longest x4 74.7 us: exchange(): return lax.all_to_all(value, axes, split_axis=0, concat_axis=0, tiled=True)]
    pallas_call x0 -> x2, Pallas kernels: none -> 27.6 us  [the longest x1 26.2 us: shards(): pl.pallas_call(basis_kernel, out_shape=(jax.ShapeDtypeStruct((rank, cells...]
    dot_general x8 -> x0, matrix products: 17.5 us -> none  [the longest x1 7.11 us: shards(): jnp.dot(fibers, fibers.T, precision=lax.Precision.HIGHEST, preferred_elem...]
    all_to_all x1 -> x0, waiting for transfers between devices: 16.4 us -> none  [shards(): lax.all_to_all(core_block, 'row', split_axis=0, concat_axis=2, tiled=True)]
    another operation x16 -> x0, matrix products: 9.24 us -> none  [the longest x6 5.47 us: shards(): basis = power_steps(jnp.linalg.cholesky(gram_sum), start_basis)]
    another operation x23 -> x0, local copies, waits for them, and re-layouts: 8.18 us -> none  [the longest x15 7.99 us: orthonormalize(): jax.scipy.linalg.solve_triangular(small_lower, applied.T, lower=True)]
  transfers between devices with their start and end apart: 2 -> 0, of which waited for: 2 -> 0; matrix products, arithmetic and copies ran while one was open for 1% -> 0% of each run, Pallas kernels for 0% -> 0%
where the time goes in v1:
time: 125 us
  blocking collectives  93.6 us (75%)
  Pallas kernels  27.6 us (22%)
  local copies, waits for them, and re-layouts  2.73 us (2%)
    all_to_all x4, blocking collectives, exchange(): return lax.all_to_all(value, axes, split_axis=0, concat_axis=0, tiled=True)  74.7 us
    pallas_call x1, Pallas kernels, shards(): pl.pallas_call(basis_kernel, out_shape=(jax.ShapeDtypeStruct((rank, cells...  26.2 us
    all_to_all x1, blocking collectives, shards(): core = lax.all_to_all(core, 'row', split_axis=0, concat_axis=2, tiled=True)  18.9 us

profile of v1, /device:TPU:1, one launch (start us, length us, event | category | flops | bytes accessed | tf_op | source)
XLA Modules:
  0.0 124.7 jit_solution(12737310756182826127)
XLA Ops:
  0.6 0.0 copy-start
  0.6 1.6 %copy-done = f32[512,8,128]{2,1,0:T(8,128)S(1)} copy-done((f32[512,8,128]{2,1,0:T(8,128)S(1)}, f32[512,8,128]{2,1,0:T(8,128)}, u32[]{:S(2)}) %copy-start) | copy-done | bytes 2097176
  2.2 1.4 %gram.1 = (f32[1280,128]{1,0:T(8,128)S(1)}, bf16[512,1024]{1,0:T(8,128)(2,1)S(1)}, bf16[512,1024]{1,0:T(8,128)(2,1)S(1)}) custom-call(f32[512,8,128]{2,1,0:T(8,128)S(1)} %copy-done), custom_call_target="tpu_custom_call" | custom-call | tf_op jit(solution)/shard_map/gram/pallas_call | solution.py:145
  3.7 0.0 copy-start.1
  3.7 22.7 %all_to_all.38 = f32[32,40,128]{2,1,0:T(8,128)S(1)} all-to-all(f32[32,40,128]{2,1,0:T(8,128)S(1)} %bitcast.9), channel_id=1, replica_groups=mesh['row'=16,'zh'=4,'zl'=4,'core'=2] {'row','core'}, dimensions={0} | all-to-all | bytes 1310720 | tf_op jit(solution)/shard_map/all_to_all | solution.py:134
  26.4 0.1 reduce_sum.27
  26.4 8.9 %all_to_all.39 = f32[4,40,128]{2,1,0:T(8,128)S(1)} all-to-all(f32[4,40,128]{2,1,0:T(8,128)S(1)} %broadcast_in_dim.9), channel_id=1, replica_groups=mesh['row'=16,'zh'=4,'zl'=4,'core'=2] {'zl'}, dimensions={0} | all-to-all | bytes 163840 | tf_op jit(solution)/shard_map/all_to_all | solution.py:134
  35.4 24.2 %all_to_all.40 = f32[4,40,128]{2,1,0:T(8,128)S(1)} all-to-all(f32[4,40,128]{2,1,0:T(8,128)S(1)} %broadcast_in_dim.10), channel_id=1, replica_groups=mesh['row'=16,'zh'=4,'zl'=4,'core'=2] {'zh'}, dimensions={0} | all-to-all | bytes 163840 | tf_op jit(solution)/shard_map/all_to_all | solution.py:134
  59.6 18.9 %all_to_all.41 = f32[32,40,128]{2,1,0:T(8,128)S(1)} all-to-all(f32[32,40,128]{2,1,0:T(8,128)S(1)} %broadcast_in_dim.11), channel_id=1, replica_groups=mesh['row'=16,'zh'=4,'zl'=4,'core'=2] {'row','core'}, dimensions={0} | all-to-all | bytes 1310720 | tf_op jit(solution)/shard_map/all_to_all | solution.py:134
  78.5 0.0 copy-done.1
  78.5 26.2 %basis.1 = (f32[256,8,128]{2,1,0:T(8,128)S(1)}, f32[512,256]{1,0:T(8,128)}) custom-call(f32[1280,128]{1,0:T(8,128)S(1)} %bitcast.8, f32[512,256]{1,0:T(8,128)S(1)} %copy-done.1, bf16[512,1024]{1,0:T(8,128)(2,1)S(1)} %get-tuple-element.8.high_ref, bf16[512,1024]{1,0:T(8,128)(2,1)S(1)} %get-tuple-element.9.low_ref), custom_call_target="tpu_custom_call" | custom-call | tf_op jit(solution)/shard_map/basis/pallas_call | solution.py:161
  104.7 18.9 %all_to_all.42 = f32[256,8,128]{2,1,0:T(8,128)S(1)} all-to-all(f32[256,8,128]{2,1,0:T(8,128)S(1)} %get-tuple-element.10), channel_id=1, replica_groups=mesh['row'=16,'zh'=4,'zl'=4,'core'=2] {'row'}, dimensions={0} | all-to-all | bytes 2097152 | tf_op jit(solution)/shard_map/all_to_all | solution.py:171
  123.6 1.1 copy.7
  (5 shorter events, 0.1 us)
Async XLA Ops:
  0.6 1.6 %copy-start = (f32[512,8,128]{2,1,0:T(8,128)S(1)}, f32[512,8,128]{2,1,0:T(8,128)}, u32[]{:S(2)}) copy-start(f32[512,8,128]{2,1,0:T(8,128)} %x_ref.1) | copy-start | bytes 6291460
  3.7 74.9 %copy-start.1 = (f32[512,256]{1,0:T(8,128)S(1)}, f32[512,256]{1,0:T(8,128)}, u32[]{:S(2)}) copy-start(f32[512,256]{1,0:T(8,128)} %start_ref.1) | copy-start | bytes 1572868

commit v2 on v1

v2 whole, which is shorter than its diff:
```python
import jax
import jax.numpy as jnp
from jax import lax
from jax.experimental import pallas as pl
from jax.experimental.pallas import tpu as pltpu
from jax.sharding import Mesh, PartitionSpec as P

ITERS = 2
TILE = 128
SUB = 8
NEAR = 2
NT = (((1,), (1,)), ((), ()))
NN = (((1,), (0,)), ((), ()))
PARAMS = pltpu.CompilerParams(vmem_limit_bytes=40 * 2**20)


def matmul(left, right, dims=NN):
    return lax.dot_general(
        left, right, dims, precision=lax.Precision.HIGHEST, preferred_element_type=jnp.float32
    )


def halves(value):
    high = value.astype(jnp.bfloat16)
    return high, (value - high.astype(jnp.float32)).astype(jnp.bfloat16)


def dot16(left, right, dims):
    return lax.dot_general(left, right, dims, preferred_element_type=jnp.float32)


def product(left, right):
    left_high, left_low = halves(left)
    right_high, right_low = halves(right)
    return dot16(left_high, right_high, NN) + (
        dot16(left_high, right_low, NN) + dot16(left_low, right_high, NN)
    )


def lower_tiles(count):
    return [(i, j) for i in range(count) for j in range(i + 1)]


def gram_kernel(x_ref, packed_ref, high_ref, low_ref):
    width, cells_z, cells_y = x_ref.shape
    flat = x_ref.reshape(width * cells_z, cells_y)
    for z in range(cells_z):
        high, low = halves(flat[pl.ds(z, width, stride=cells_z), :])
        high_ref[:, z * cells_y : (z + 1) * cells_y] = high
        low_ref[:, z * cells_y : (z + 1) * cells_y] = low
    side = 2 * TILE
    for i, j in lower_tiles(width // side):
        rows, columns = pl.ds(i * side, side), pl.ds(j * side, side)
        block = dot16(high_ref[rows, :], high_ref[columns, :], NT)
        cross = dot16(high_ref[rows, :], low_ref[columns, :], NT)
        if i == j:
            block = block + (cross + cross.T)
        else:
            block = block + (cross + dot16(low_ref[rows, :], high_ref[columns, :], NT))
        for place, (a, b) in enumerate(lower_tiles(width // TILE)):
            if (a // 2, b // 2) == (i, j):
                ra, rb = (a % 2) * TILE, (b % 2) * TILE
                packed_ref[place * TILE : (place + 1) * TILE, :] = block[ra : ra + TILE, rb : rb + TILE]


def spread_row(tile, k):
    return jnp.broadcast_to(tile[k : k + 1, :], tile.shape)


def spread_column(tile, k):
    return jnp.broadcast_to(tile[:, k : k + 1], tile.shape)


def total_of(terms):
    while len(terms) > 1:
        terms = [sum(terms[i + 1 : i + 2], terms[i]) for i in range(0, len(terms), 2)]
    return terms[0]


def inverse_factors(matrices, depth):
    size = matrices[0].shape[0]
    count = size // SUB
    sub = lax.broadcasted_iota(jnp.int32, (SUB, size), 0)
    lane = lax.broadcasted_iota(jnp.int32, (SUB, size), 1)
    zero = jnp.zeros((SUB, size), jnp.float32)
    all_tiles = [[m[SUB * t : SUB * (t + 1), :] for t in range(count)] for m in matrices]
    all_done = [[] for _ in matrices]
    for t in range(0, count, depth):
        first, across = SUB * t, SUB * depth
        panel = (lane >= first) & (lane < first + across)
        for tiles, done in zip(all_tiles, all_done):
            own = range(depth)
            columns = [
                [spread_column(tiles[t + q], first + k) for k in range(across)] for q in own
            ]
            rest = [
                jnp.where(
                    panel, jnp.where(lane - first - SUB * q == sub, 1.0, 0.0), tiles[t + q]
                )
                for q in own
            ]
            forward, pivots, scales = list(rest), [None] * depth, [None] * depth
            for k in range(across):
                p, row = divmod(k, SUB)
                here = sub == row
                scale = 1.0 / spread_row(columns[p][k], row)
                factors = [columns[q][k] for q in own]
                factors[p] = jnp.where(here, 0.0, factors[p])
                if row:
                    forward[p] = jnp.where(sub >= row, rest[p], forward[p])
                    pivots[p] = jnp.where(here, columns[p][k], pivots[p])
                    scales[p] = jnp.where(here, scale, scales[p])
                else:
                    forward[p], pivots[p], scales[p] = rest[p], columns[p][k], scale
                for j in range(k + 1, across):
                    spread = spread_row(columns[p][j], row)
                    for q in own:
                        columns[q][j] = columns[q][j] - (factors[q] * spread) * scale
                spread = spread_row(rest[p], row)
                for q in own:
                    rest[q] = rest[q] - (factors[q] * spread) * scale
            solved = [rest[q] * scales[q] for q in own]
            rows = [spread_row(solved[k // SUB], k % SUB) for k in range(across)]
            near = t + depth
            far = min(near + NEAR, count)
            for i in range(near, far):
                change = [spread_column(tiles[i], first + k) * rows[k] for k in range(across)]
                tiles[i] = jnp.where(panel, 0.0, tiles[i]) - total_of(change)
            for q in own:
                kept = lane <= first + SUB * q + sub
                done.append(jnp.where(kept, forward[q] * lax.rsqrt(pivots[q]), 0.0))
            if far < count:
                right = [solved[i - t] if i - t in own else zero for i in range(count)]
                change = matmul(jnp.concatenate(tiles[far:], 0), jnp.concatenate(right, 0))
                for i in range(far, count):
                    place = SUB * (i - far)
                    tiles[i] = jnp.where(panel, 0.0, tiles[i]) - change[place : place + SUB]
    return [jnp.concatenate(done, axis=0) for done in all_done]


def basis_kernel(
    packed_ref, start_ref, high_ref, low_ref, core_ref, basis_ref, *scratch
):
    gram_high, gram_low, current_ref, applied_ref, rest_ref = scratch
    width = start_ref.shape[0]
    rank, cells_z, cells_y = core_ref.shape
    half = rank // 2
    for place, (a, b) in enumerate(lower_tiles(width // TILE)):
        tile = packed_ref[place * TILE : (place + 1) * TILE, :]
        for i, j, value in ((a, b, tile), (b, a, tile.T))[: 1 + (a != b)]:
            rows, columns = pl.ds(i * TILE, TILE), pl.ds(j * TILE, TILE)
            gram_high[rows, columns], gram_low[rows, columns] = halves(value)

    def times_gram(sweep, part):
        high, low = halves(current_ref[sweep, part])
        applied_ref[sweep, part] = dot16(high, gram_high[...], NN) + (
            dot16(high, gram_low[...], NN) + dot16(low, gram_high[...], NN)
        )

    def inner(sweep, left, right):
        return matmul(applied_ref[sweep, left], applied_ref[sweep, right], NT)

    def first_half(sweep, inverse):
        current_ref[sweep + 1, 0] = product(inverse, applied_ref[sweep, 0])

    def second_matrix(sweep, inverse):
        below = matmul(inner(sweep, 1, 0), inverse, NT)
        rest_ref[sweep] = applied_ref[sweep, 1] - matmul(below, current_ref[sweep + 1, 0])
        return inner(sweep, 1, 1) - matmul(below, below, NT)

    def second_half(sweep, inverse):
        current_ref[sweep + 1, 1] = product(inverse, rest_ref[sweep])

    def write(part):
        value = current_ref[ITERS, part]
        basis_ref[:, part * half : (part + 1) * half] = value.T
        high, low = halves(value)
        flat = core_ref.reshape(rank * cells_z, cells_y)
        for z in range(0, cells_z, 2):
            columns = pl.ds(z * cells_y, 2 * cells_y)
            block = dot16(high, high_ref[:, columns], NN) + (
                dot16(high, low_ref[:, columns], NN) + dot16(low, high_ref[:, columns], NN)
            )
            for q in range(2):
                rows = pl.ds(part * half * cells_z + z + q, half, stride=cells_z)
                flat[rows, :] = block[:, q * cells_y : (q + 1) * cells_y]

    for part in range(2):
        current_ref[0, part] = start_ref[:, part * half : (part + 1) * half].T
        times_gram(0, part)
    (inverse,) = inverse_factors([inner(0, 0, 0)], 2)
    for sweep in range(ITERS):
        first_half(sweep, inverse)
        matrix = second_matrix(sweep, inverse)
        if sweep + 1 < ITERS:
            times_gram(sweep + 1, 0)
            second, inverse = inverse_factors([matrix, inner(sweep + 1, 0, 0)], 1)
            second_half(sweep, second)
            times_gram(sweep + 1, 1)
        else:
            write(0)
            (second,) = inverse_factors([matrix], 2)
            second_half(sweep, second)
            write(1)


def exchange(value, axes):
    return lax.all_to_all(value, axes, split_axis=0, concat_axis=0, tiled=True)


def sum_over(value, axes, members):
    return exchange(jnp.broadcast_to(value, (members, *value.shape)), axes).sum(axis=0)


def shards(species, start_basis):
    width, cells_z, cells_y = species.shape
    rank = start_basis.shape[1]
    tiles = len(lower_tiles(width // TILE))
    packed, high, low = pl.pallas_call(
        gram_kernel,
        out_shape=(
            jax.ShapeDtypeStruct((tiles * TILE, TILE), jnp.float32),
            jax.ShapeDtypeStruct((width, cells_z * cells_y), jnp.bfloat16),
            jax.ShapeDtypeStruct((width, cells_z * cells_y), jnp.bfloat16),
        ),
        compiler_params=PARAMS,
        name="gram",
    )(species)
    plane = ("row", "core")
    members = lax.axis_size(plane)
    part = exchange(packed.reshape(members, -1, TILE), plane).sum(axis=0)
    part = sum_over(part, ("zh", "zl"), lax.axis_size(("zh", "zl")))
    packed = exchange(jnp.broadcast_to(part, (members, *part.shape)), plane)
    core, basis = pl.pallas_call(
        basis_kernel,
        out_shape=(
            jax.ShapeDtypeStruct((rank, cells_z, cells_y), jnp.float32),
            jax.ShapeDtypeStruct((width, rank), jnp.float32),
        ),
        scratch_shapes=[
            pltpu.VMEM((width, width), jnp.bfloat16),
            pltpu.VMEM((width, width), jnp.bfloat16),
            pltpu.VMEM((ITERS + 1, 2, rank // 2, width), jnp.float32),
            pltpu.VMEM((ITERS, 2, rank // 2, width), jnp.float32),
            pltpu.VMEM((ITERS, rank // 2, width), jnp.float32),
        ],
        compiler_params=PARAMS,
        name="basis",
    )(packed.reshape(-1, TILE), start_basis, high, low)
    core = lax.all_to_all(core, "row", split_axis=0, concat_axis=2, tiled=True)
    return core, basis


def solution(mesh):
    rows, columns = mesh.devices.shape
    fine = Mesh(mesh.devices.reshape(rows, columns // 8, 4, 2), ("row", "zh", "zl", "core"))
    split = ("zh", "zl", "core")
    return jax.shard_map(
        shards,
        mesh=fine,
        in_specs=(P(None, split, "row"), P()),
        out_specs=(P("row", split, None), P()),
        check_vma=False,
    )
```

time: 125 us -> 115 us (0.920)
  Pallas kernels: 27.6 us -> 17.9 us
    pallas_call x1, Pallas kernels: 26.2 us -> 16.4 us  [shards(): pl.pallas_call(basis_kernel, out_shape=(jax.ShapeDtypeStruct((rank, cells...]
    all_to_all x4 -> x3, blocking collectives: 74.7 us -> 74.2 us  [exchange(): return lax.all_to_all(value, axes, split_axis=0, concat_axis=0, tiled=True)]
where the time goes in v2:
time: 115 us; the launch traced here: 114 us
  blocking collectives  93.1 us (81%)
  Pallas kernels  17.9 us (16%)
  local copies, waits for them, and re-layouts  2.73 us (2%)
    all_to_all x3, blocking collectives, exchange(): return lax.all_to_all(value, axes, split_axis=0, concat_axis=0, tiled=True)  74.2 us
    all_to_all x1, blocking collectives, shards(): core = lax.all_to_all(core, 'row', split_axis=0, concat_axis=2, tiled=True)  18.9 us
    pallas_call x1, Pallas kernels, shards(): pl.pallas_call(basis_kernel, out_shape=(jax.ShapeDtypeStruct((rank, cells...  16.4 us

profile of v2, /device:TPU:1, one launch (start us, length us, event | category | flops | bytes accessed | tf_op | source)
XLA Modules:
  0.0 114.4 jit_solution(17172007486771808386)
XLA Ops:
  0.6 0.0 copy-start
  0.6 1.6 %copy-done = f32[512,8,128]{2,1,0:T(8,128)S(1)} copy-done((f32[512,8,128]{2,1,0:T(8,128)S(1)}, f32[512,8,128]{2,1,0:T(8,128)}, u32[]{:S(2)}) %copy-start) | copy-done | bytes 2097176
  2.2 1.4 %gram.1 = (f32[1280,128]{1,0:T(8,128)S(1)}, bf16[512,1024]{1,0:T(8,128)(2,1)S(1)}, bf16[512,1024]{1,0:T(8,128)(2,1)S(1)}) custom-call(f32[512,8,128]{2,1,0:T(8,128)S(1)} %copy-done), custom_call_target="tpu_custom_call" | custom-call | tf_op jit(solution)/shard_map/gram/pallas_call | solution.py:219
  3.7 22.6 %all_to_all.33 = f32[32,40,128]{2,1,0:T(8,128)S(1)} all-to-all(f32[32,40,128]{2,1,0:T(8,128)S(1)} %bitcast.9), channel_id=1, replica_groups=mesh['row'=16,'zh'=4,'zl'=4,'core'=2] {'row','core'}, dimensions={0} | all-to-all | bytes 1310720 | tf_op jit(solution)/shard_map/all_to_all | solution.py:208
  26.2 0.0 copy-start.1
  26.2 0.1 reduce_sum.18
  26.3 31.8 %all_to_all.34 = f32[16,40,128]{2,1,0:T(8,128)S(1)} all-to-all(f32[16,40,128]{2,1,0:T(8,128)S(1)} %broadcast_in_dim.6), channel_id=1, replica_groups=mesh['row'=16,'zh'=4,'zl'=4,'core'=2] {'zh','zl'}, dimensions={0} | all-to-all | bytes 655360 | tf_op jit(solution)/shard_map/all_to_all | solution.py:208
  58.2 19.9 %all_to_all.35 = f32[32,40,128]{2,1,0:T(8,128)S(1)} all-to-all(f32[32,40,128]{2,1,0:T(8,128)S(1)} %broadcast_in_dim.7), channel_id=1, replica_groups=mesh['row'=16,'zh'=4,'zl'=4,'core'=2] {'row','core'}, dimensions={0} | all-to-all | bytes 1310720 | tf_op jit(solution)/shard_map/all_to_all | solution.py:208
  78.1 0.0 copy-done.1
  78.1 16.4 %basis.1 = (f32[256,8,128]{2,1,0:T(8,128)S(1)}, f32[512,256]{1,0:T(8,128)}) custom-call(f32[1280,128]{1,0:T(8,128)S(1)} %bitcast.8, f32[512,256]{1,0:T(8,128)S(1)} %copy-done.1, bf16[512,1024]{1,0:T(8,128)(2,1)S(1)} %get-tuple-element.8.high_ref, bf16[512,1024]{1,0:T(8,128)(2,1)S(1)} %get-tuple-element.9.low_ref), custom_call_target="tpu_custom_call" | custom-call | tf_op jit(solution)/shard_map/basis/pallas_call | solution.py:234
  94.5 18.9 %all_to_all.36 = f32[256,8,128]{2,1,0:T(8,128)S(1)} all-to-all(f32[256,8,128]{2,1,0:T(8,128)S(1)} %get-tuple-element.10), channel_id=1, replica_groups=mesh['row'=16,'zh'=4,'zl'=4,'core'=2] {'row'}, dimensions={0} | all-to-all | bytes 2097152 | tf_op jit(solution)/shard_map/all_to_all | solution.py:250
  113.4 1.1 copy.7
  (3 shorter events, 0.1 us)
Async XLA Ops:
  0.6 1.6 %copy-start = (f32[512,8,128]{2,1,0:T(8,128)S(1)}, f32[512,8,128]{2,1,0:T(8,128)}, u32[]{:S(2)}) copy-start(f32[512,8,128]{2,1,0:T(8,128)} %x_ref.1) | copy-start | bytes 6291460
  26.2 51.8 %copy-start.1 = (f32[512,256]{1,0:T(8,128)S(1)}, f32[512,256]{1,0:T(8,128)}, u32[]{:S(2)}) copy-start(f32[512,256]{1,0:T(8,128)} %start_ref.1) | copy-start | bytes 1572868

commit v3 on v2

--- a/solution.py
+++ b/solution.py
@@ -14,12 +14,6 @@
 PARAMS = pltpu.CompilerParams(vmem_limit_bytes=40 * 2**20)
 
 
-def matmul(left, right, dims=NN):
-    return lax.dot_general(
-        left, right, dims, precision=lax.Precision.HIGHEST, preferred_element_type=jnp.float32
-    )
-
-
 def halves(value):
     high = value.astype(jnp.bfloat16)
     return high, (value - high.astype(jnp.float32)).astype(jnp.bfloat16)
@@ -29,11 +23,11 @@
     return lax.dot_general(left, right, dims, preferred_element_type=jnp.float32)
 
 
-def product(left, right):
+def matmul(left, right, dims=NN):
     left_high, left_low = halves(left)
     right_high, right_low = halves(right)
-    return dot16(left_high, right_high, NN) + (
-        dot16(left_high, right_low, NN) + dot16(left_low, right_high, NN)
+    return dot16(left_high, right_high, dims) + (
+        dot16(left_high, right_low, dims) + dot16(left_low, right_high, dims)
     )
 
 
@@ -161,7 +155,7 @@
         return matmul(applied_ref[sweep, left], applied_ref[sweep, right], NT)
 
     def first_half(sweep, inverse):
-        current_ref[sweep + 1, 0] = product(inverse, applied_ref[sweep, 0])
+        current_ref[sweep + 1, 0] = matmul(inverse, applied_ref[sweep, 0])
 
     def second_matrix(sweep, inverse):
         below = matmul(inner(sweep, 1, 0), inverse, NT)
@@ -169,7 +163,7 @@
         return inner(sweep, 1, 1) - matmul(below, below, NT)
 
     def second_half(sweep, inverse):
-        current_ref[sweep + 1, 1] = product(inverse, rest_ref[sweep])
+        current_ref[sweep + 1, 1] = matmul(inverse, rest_ref[sweep])
 
     def write(part):
         value = current_ref[ITERS, part]
@@ -194,7 +188,7 @@
         matrix = second_matrix(sweep, inverse)
         if sweep + 1 < ITERS:
             times_gram(sweep + 1, 0)
-            second, inverse = inverse_factors([matrix, inner(sweep + 1, 0, 0)], 1)
+            second, inverse = inverse_factors([matrix, inner(sweep + 1, 0, 0)], 2)
             second_half(sweep, second)
             times_gram(sweep + 1, 1)
         else:

time: 115 us -> 112 us (0.974)
  Pallas kernels: 17.9 us -> 15.3 us
    pallas_call x1, Pallas kernels: 16.4 us -> 13.9 us  [shards(): pl.pallas_call(basis_kernel, out_shape=(jax.ShapeDtypeStruct((rank, cells...]
where the time goes in v3:
time: 112 us
  blocking collectives  93.1 us (83%)
  Pallas kernels  15.3 us (14%)
  local copies, waits for them, and re-layouts  2.73 us (2%)
    all_to_all x3, blocking collectives, exchange(): return lax.all_to_all(value, axes, split_axis=0, concat_axis=0, tiled=True)  74.2 us
    all_to_all x1, blocking collectives, shards(): core = lax.all_to_all(core, 'row', split_axis=0, concat_axis=2, tiled=True)  18.9 us
    pallas_call x1, Pallas kernels, shards(): pl.pallas_call(basis_kernel, out_shape=(jax.ShapeDtypeStruct((rank, cells...  13.9 us

profile of v3, /device:TPU:1, one launch (start us, length us, event | category | flops | bytes accessed | tf_op | source)
XLA Modules:
  0.0 111.9 jit_solution(12992385590384003789)
XLA Ops:
  0.6 0.0 copy-start
  0.6 1.6 %copy-done = f32[512,8,128]{2,1,0:T(8,128)S(1)} copy-done((f32[512,8,128]{2,1,0:T(8,128)S(1)}, f32[512,8,128]{2,1,0:T(8,128)}, u32[]{:S(2)}) %copy-start) | copy-done | bytes 2097176
  2.2 1.4 %gram.1 = (f32[1280,128]{1,0:T(8,128)S(1)}, bf16[512,1024]{1,0:T(8,128)(2,1)S(1)}, bf16[512,1024]{1,0:T(8,128)(2,1)S(1)}) custom-call(f32[512,8,128]{2,1,0:T(8,128)S(1)} %copy-done), custom_call_target="tpu_custom_call" | custom-call | tf_op jit(solution)/shard_map/gram/pallas_call | solution.py:213
  3.7 22.6 %all_to_all.33 = f32[32,40,128]{2,1,0:T(8,128)S(1)} all-to-all(f32[32,40,128]{2,1,0:T(8,128)S(1)} %bitcast.9), channel_id=1, replica_groups=mesh['row'=16,'zh'=4,'zl'=4,'core'=2] {'row','core'}, dimensions={0} | all-to-all | bytes 1310720 | tf_op jit(solution)/shard_map/all_to_all | solution.py:202
  26.2 0.0 copy-start.1
  26.2 0.1 reduce_sum.18
  26.3 31.8 %all_to_all.34 = f32[16,40,128]{2,1,0:T(8,128)S(1)} all-to-all(f32[16,40,128]{2,1,0:T(8,128)S(1)} %broadcast_in_dim.6), channel_id=1, replica_groups=mesh['row'=16,'zh'=4,'zl'=4,'core'=2] {'zh','zl'}, dimensions={0} | all-to-all | bytes 655360 | tf_op jit(solution)/shard_map/all_to_all | solution.py:202
  58.2 19.9 %all_to_all.35 = f32[32,40,128]{2,1,0:T(8,128)S(1)} all-to-all(f32[32,40,128]{2,1,0:T(8,128)S(1)} %broadcast_in_dim.7), channel_id=1, replica_groups=mesh['row'=16,'zh'=4,'zl'=4,'core'=2] {'row','core'}, dimensions={0} | all-to-all | bytes 1310720 | tf_op jit(solution)/shard_map/all_to_all | solution.py:202
  78.1 0.0 copy-done.1
  78.1 13.9 %basis.1 = (f32[256,8,128]{2,1,0:T(8,128)S(1)}, f32[512,256]{1,0:T(8,128)}) custom-call(f32[1280,128]{1,0:T(8,128)S(1)} %bitcast.8, f32[512,256]{1,0:T(8,128)S(1)} %copy-done.1, bf16[512,1024]{1,0:T(8,128)(2,1)S(1)} %get-tuple-element.8.high_ref, bf16[512,1024]{1,0:T(8,128)(2,1)S(1)} %get-tuple-element.9.low_ref), custom_call_target="tpu_custom_call" | custom-call | tf_op jit(solution)/shard_map/basis/pallas_call | solution.py:228
  92.0 18.9 %all_to_all.36 = f32[256,8,128]{2,1,0:T(8,128)S(1)} all-to-all(f32[256,8,128]{2,1,0:T(8,128)S(1)} %get-tuple-element.10), channel_id=1, replica_groups=mesh['row'=16,'zh'=4,'zl'=4,'core'=2] {'row'}, dimensions={0} | all-to-all | bytes 2097152 | tf_op jit(solution)/shard_map/all_to_all | solution.py:244
  110.8 1.1 copy.7
  (3 shorter events, 0.1 us)
Async XLA Ops:
  0.6 1.6 %copy-start = (f32[512,8,128]{2,1,0:T(8,128)S(1)}, f32[512,8,128]{2,1,0:T(8,128)}, u32[]{:S(2)}) copy-start(f32[512,8,128]{2,1,0:T(8,128)} %x_ref.1) | copy-start | bytes 6291460
  26.2 51.8 %copy-start.1 = (f32[512,256]{1,0:T(8,128)S(1)}, f32[512,256]{1,0:T(8,128)}, u32[]{:S(2)}) copy-start(f32[512,256]{1,0:T(8,128)} %start_ref.1) | copy-start | bytes 1572868

commit v4 on v3

--- a/solution.py
+++ b/solution.py
@@ -31,30 +31,40 @@
     )
 
 
-def lower_tiles(count):
-    return [(i, j) for i in range(count) for j in range(i + 1)]
+def below_tiles(count):
+    return [(i, j) for i in range(count) for j in range(i)]
+
+
+def diagonal_places(count, i):
+    half = TILE // 2
+    first = len(below_tiles(count)) * TILE + i // 2 * 3 * half
+    return pl.ds(first + i % 2 * 2 * half, half), pl.ds(first + half, half)
 
 
 def gram_kernel(x_ref, packed_ref, high_ref, low_ref):
     width, cells_z, cells_y = x_ref.shape
     flat = x_ref.reshape(width * cells_z, cells_y)
     for z in range(cells_z):
-        high, low = halves(flat[pl.ds(z, width, stride=cells_z), :])
-        high_ref[:, z * cells_y : (z + 1) * cells_y] = high
-        low_ref[:, z * cells_y : (z + 1) * cells_y] = low
-    side = 2 * TILE
-    for i, j in lower_tiles(width // side):
-        rows, columns = pl.ds(i * side, side), pl.ds(j * side, side)
-        block = dot16(high_ref[rows, :], high_ref[columns, :], NT)
-        cross = dot16(high_ref[rows, :], low_ref[columns, :], NT)
-        if i == j:
-            block = block + (cross + cross.T)
-        else:
-            block = block + (cross + dot16(low_ref[rows, :], high_ref[columns, :], NT))
-        for place, (a, b) in enumerate(lower_tiles(width // TILE)):
-            if (a // 2, b // 2) == (i, j):
-                ra, rb = (a % 2) * TILE, (b % 2) * TILE
-                packed_ref[place * TILE : (place + 1) * TILE, :] = block[ra : ra + TILE, rb : rb + TILE]
+        columns = pl.ds(z * cells_y, cells_y)
+        high_ref[:, columns], low_ref[:, columns] = halves(
+            flat[pl.ds(z, width, stride=cells_z), :]
+        )
+    count = width // TILE
+    for step in range(count):
+        rows, upto = pl.ds(step * TILE, TILE), pl.ds(0, (step + 1) * TILE)
+        block = dot16(high_ref[rows, :], high_ref[upto, :], NT) + (
+            dot16(high_ref[rows, :], low_ref[upto, :], NT)
+            + dot16(low_ref[rows, :], high_ref[upto, :], NT)
+        )
+        for place, (a, b) in enumerate(below_tiles(count)):
+            if a == step:
+                packed_ref[pl.ds(place * TILE, TILE), :] = block[:, b * TILE : (b + 1) * TILE]
+        tile = block[:, step * TILE :]
+        top, bottom = tile[: TILE // 2], tile[TILE // 2 :]
+        left = lax.broadcasted_iota(jnp.int32, top.shape, 1) < TILE // 2
+        own, shared = diagonal_places(count, step)
+        packed_ref[own, :] = jnp.where(left, top, bottom)
+        packed_ref[shared, :] = jnp.where(left, packed_ref[shared, :], top) if step % 2 else bottom
 
 
 def spread_row(tile, k):
@@ -139,11 +149,27 @@
     width = start_ref.shape[0]
     rank, cells_z, cells_y = core_ref.shape
     half = rank // 2
-    for place, (a, b) in enumerate(lower_tiles(width // TILE)):
+    count = width // TILE
+
+    def keep(i, j, value):
+        rows, columns = pl.ds(i * TILE, TILE), pl.ds(j * TILE, TILE)
+        gram_high[rows, columns], gram_low[rows, columns] = halves(value)
+
+    for place, (a, b) in enumerate(below_tiles(count)):
         tile = packed_ref[place * TILE : (place + 1) * TILE, :]
-        for i, j, value in ((a, b, tile), (b, a, tile.T))[: 1 + (a != b)]:
-            rows, columns = pl.ds(i * TILE, TILE), pl.ds(j * TILE, TILE)
-            gram_high[rows, columns], gram_low[rows, columns] = halves(value)
+        keep(a, b, tile)
+        keep(b, a, tile.T)
+    for i in range(count):
+        own, shared = (packed_ref[rows, :] for rows in diagonal_places(count, i))
+        left = lax.broadcasted_iota(jnp.int32, own.shape, 1) < TILE // 2
+        if i % 2:
+            tile = jnp.concatenate([jnp.where(left, own, shared), own], axis=0)
+        else:
+            tile = jnp.concatenate([own, jnp.where(left, shared, own)], axis=0)
+        row = lax.broadcasted_iota(jnp.int32, tile.shape, 0) < TILE // 2
+        column = lax.broadcasted_iota(jnp.int32, tile.shape, 1) < TILE // 2
+        missing = (column if i % 2 else row) & (row != column)
+        keep(i, i, jnp.where(missing, tile.T, tile))
 
     def times_gram(sweep, part):
         high, low = halves(current_ref[sweep, part])
@@ -209,11 +235,12 @@
 def shards(species, start_basis):
     width, cells_z, cells_y = species.shape
     rank = start_basis.shape[1]
-    tiles = len(lower_tiles(width // TILE))
+    tiles = width // TILE
+    packed_rows = (len(below_tiles(tiles)) + tiles * 3 // 4) * TILE
     packed, high, low = pl.pallas_call(
         gram_kernel,
         out_shape=(
-            jax.ShapeDtypeStruct((tiles * TILE, TILE), jnp.float32),
+            jax.ShapeDtypeStruct((packed_rows, TILE), jnp.float32),
             jax.ShapeDtypeStruct((width, cells_z * cells_y), jnp.bfloat16),
             jax.ShapeDtypeStruct((width, cells_z * cells_y), jnp.bfloat16),
         ),
@@ -222,7 +249,7 @@
     )(species)
     plane = ("row", "core")
     members = lax.axis_size(plane)
-    part = exchange(packed.reshape(members, -1, TILE), plane).sum(axis=0)
+    part = exchange(packed.reshape(members, -1, 4, TILE), plane).sum(axis=0)
     part = sum_over(part, ("zh", "zl"), lax.axis_size(("zh", "zl")))
     packed = exchange(jnp.broadcast_to(part, (members, *part.shape)), plane)
     core, basis = pl.pallas_call(

time: 112 us -> 111 us (level)
  blocking collectives: 93.1 us -> 90.2 us
  Pallas kernels: 15.3 us -> 16.7 us
    all_to_all x3, blocking collectives: 74.2 us -> 71.4 us  [exchange(): return lax.all_to_all(value, axes, split_axis=0, concat_axis=0, tiled=True)]
    pallas_call x1, Pallas kernels: 1.42 us -> 2.73 us  [shards(): pl.pallas_call(gram_kernel, out_shape=(jax.ShapeDtypeStruct((packed_rows,...]
where the time goes in v4:
time: 111 us
  blocking collectives  90.2 us (81%)
  Pallas kernels  16.7 us (15%)
  local copies, waits for them, and re-layouts  2.78 us (3%)
    all_to_all x3, blocking collectives, exchange(): return lax.all_to_all(value, axes, split_axis=0, concat_axis=0, tiled=True)  71.4 us
    all_to_all x1, blocking collectives, shards(): core = lax.all_to_all(core, 'row', split_axis=0, concat_axis=2, tiled=True)  18.8 us
    pallas_call x1, Pallas kernels, shards(): pl.pallas_call(basis_kernel, out_shape=(jax.ShapeDtypeStruct((rank, cells...  14 us
    pallas_call x1, Pallas kernels, shards(): pl.pallas_call(gram_kernel, out_shape=(jax.ShapeDtypeStruct((packed_rows,...  2.73 us

profile of v4, /device:TPU:1, one launch (start us, length us, event | category | flops | bytes accessed | tf_op | source)
XLA Modules:
  0.0 110.5 jit_solution(15173050206767337066)
XLA Ops:
  0.6 0.0 copy-start
  0.6 1.6 %copy-done = f32[512,8,128]{2,1,0:T(8,128)S(1)} copy-done((f32[512,8,128]{2,1,0:T(8,128)S(1)}, f32[512,8,128]{2,1,0:T(8,128)}, u32[]{:S(2)}) %copy-start) | copy-done | bytes 2097176
  2.2 2.7 %gram.1 = (f32[1152,128]{1,0:T(8,128)S(1)}, bf16[512,1024]{1,0:T(8,128)(2,1)S(1)}, bf16[512,1024]{1,0:T(8,128)(2,1)S(1)}) custom-call(f32[512,8,128]{2,1,0:T(8,128)S(1)} %copy-done), custom_call_target="tpu_custom_call" | custom-call | tf_op jit(solution)/shard_map/gram/pallas_call | solution.py:240
  5.0 21.9 %all_to_all.33 = f32[32,9,4,128]{3,2,1,0:T(4,128)S(1)} all-to-all(f32[32,9,4,128]{3,2,1,0:T(4,128)S(1)} %bitcast.9), channel_id=1, replica_groups=mesh['row'=16,'zh'=4,'zl'=4,'core'=2] {'row','core'}, dimensions={0} | all-to-all | bytes 1179648 | tf_op jit(solution)/shard_map/all_to_all | solution.py:228
  26.9 0.0 copy-start.1
  26.9 0.1 reduce_sum.18
  27.0 29.8 %all_to_all.34 = f32[16,9,4,128]{3,2,1,0:T(4,128)S(1)} all-to-all(f32[16,9,4,128]{3,2,1,0:T(4,128)S(1)} %broadcast_in_dim.6), channel_id=1, replica_groups=mesh['row'=16,'zh'=4,'zl'=4,'core'=2] {'zh','zl'}, dimensions={0} | all-to-all | bytes 589824 | tf_op jit(solution)/shard_map/all_to_all | solution.py:228
  56.9 0.1 reduce_sum.19
  56.9 0.1 broadcast_in_dim.7
  57.0 19.7 %all_to_all.35 = f32[32,9,4,128]{3,2,1,0:T(4,128)S(1)} all-to-all(f32[32,9,4,128]{3,2,1,0:T(4,128)S(1)} %broadcast_in_dim.7), channel_id=1, replica_groups=mesh['row'=16,'zh'=4,'zl'=4,'core'=2] {'row','core'}, dimensions={0} | all-to-all | bytes 1179648 | tf_op jit(solution)/shard_map/all_to_all | solution.py:228
  76.7 0.0 copy-done.1
  76.7 14.0 %basis.1 = (f32[256,8,128]{2,1,0:T(8,128)S(1)}, f32[512,256]{1,0:T(8,128)}) custom-call(f32[1152,128]{1,0:T(8,128)S(1)} %bitcast.8, f32[512,256]{1,0:T(8,128)S(1)} %copy-done.1, bf16[512,1024]{1,0:T(8,128)(2,1)S(1)} %get-tuple-element.8.high_ref, bf16[512,1024]{1,0:T(8,128)(2,1)S(1)} %get-tuple-element.9.low_ref), custom_call_target="tpu_custom_call" | custom-call | tf_op jit(solution)/shard_map/basis/pallas_call | solution.py:255
  90.7 18.8 %all_to_all.36 = f32[256,8,128]{2,1,0:T(8,128)S(1)} all-to-all(f32[256,8,128]{2,1,0:T(8,128)S(1)} %get-tuple-element.10), channel_id=1, replica_groups=mesh['row'=16,'zh'=4,'zl'=4,'core'=2] {'row'}, dimensions={0} | all-to-all | bytes 2097152 | tf_op jit(solution)/shard_map/all_to_all | solution.py:271
  109.5 1.1 copy.10
  (1 shorter events, 0.0 us)
Async XLA Ops:
  0.6 1.6 %copy-start = (f32[512,8,128]{2,1,0:T(8,128)S(1)}, f32[512,8,128]{2,1,0:T(8,128)}, u32[]{:S(2)}) copy-start(f32[512,8,128]{2,1,0:T(8,128)} %x_ref.1) | copy-start | bytes 6291460
  26.9 49.8 %copy-start.1 = (f32[512,256]{1,0:T(8,128)S(1)}, f32[512,256]{1,0:T(8,128)}, u32[]{:S(2)}) copy-start(f32[512,256]{1,0:T(8,128)} %start_ref.1) | copy-start | bytes 1572868

commit v5 on v4

--- a/solution.py
+++ b/solution.py
@@ -49,22 +49,29 @@
         high_ref[:, columns], low_ref[:, columns] = halves(
             flat[pl.ds(z, width, stride=cells_z), :]
         )
-    count = width // TILE
-    for step in range(count):
-        rows, upto = pl.ds(step * TILE, TILE), pl.ds(0, (step + 1) * TILE)
-        block = dot16(high_ref[rows, :], high_ref[upto, :], NT) + (
-            dot16(high_ref[rows, :], low_ref[upto, :], NT)
-            + dot16(low_ref[rows, :], high_ref[upto, :], NT)
-        )
+    count, side = width // TILE, 2 * TILE
+    for i, j in below_tiles(width // side) + [(i, i) for i in range(width // side)]:
+        rows, columns = pl.ds(i * side, side), pl.ds(j * side, side)
+        block = dot16(high_ref[rows, :], high_ref[columns, :], NT)
+        cross = dot16(high_ref[rows, :], low_ref[columns, :], NT)
+        if i == j:
+            block = block + (cross + cross.T)
+        else:
+            block = block + (cross + dot16(low_ref[rows, :], high_ref[columns, :], NT))
         for place, (a, b) in enumerate(below_tiles(count)):
-            if a == step:
-                packed_ref[pl.ds(place * TILE, TILE), :] = block[:, b * TILE : (b + 1) * TILE]
-        tile = block[:, step * TILE :]
-        top, bottom = tile[: TILE // 2], tile[TILE // 2 :]
-        left = lax.broadcasted_iota(jnp.int32, top.shape, 1) < TILE // 2
-        own, shared = diagonal_places(count, step)
-        packed_ref[own, :] = jnp.where(left, top, bottom)
-        packed_ref[shared, :] = jnp.where(left, packed_ref[shared, :], top) if step % 2 else bottom
+            if (a // 2, b // 2) == (i, j):
+                p, q = a % 2 * TILE, b % 2 * TILE
+                packed_ref[pl.ds(place * TILE, TILE), :] = block[p : p + TILE, q : q + TILE]
+        if i != j:
+            continue
+        half = TILE // 2
+        left = lax.broadcasted_iota(jnp.int32, (half, TILE), 1) < half
+        first, second = block[:TILE, :TILE], block[TILE:, TILE:]
+        own, shared = diagonal_places(count, 2 * i)
+        packed_ref[own, :] = jnp.where(left, first[:half], first[half:])
+        packed_ref[shared, :] = jnp.where(left, first[half:], second[:half])
+        own, shared = diagonal_places(count, 2 * i + 1)
+        packed_ref[own, :] = jnp.where(left, second[:half], second[half:])
 
 
 def spread_row(tile, k):

time: 111 us -> 110 us (level)
  no operation moved by 1% of the time
where the time goes in v5:
time: 110 us; the launch traced here: 109 us
  blocking collectives  90.2 us (82%)
  Pallas kernels  15.6 us (14%)
  local copies, waits for them, and re-layouts  2.78 us (3%)
    all_to_all x3, blocking collectives, exchange(): return lax.all_to_all(value, axes, split_axis=0, concat_axis=0, tiled=True)  71.4 us
    all_to_all x1, blocking collectives, shards(): core = lax.all_to_all(core, 'row', split_axis=0, concat_axis=2, tiled=True)  18.8 us
    pallas_call x1, Pallas kernels, shards(): pl.pallas_call(basis_kernel, out_shape=(jax.ShapeDtypeStruct((rank, cells...  14 us

profile of v5, /device:TPU:1, one launch (start us, length us, event | category | flops | bytes accessed | tf_op | source)
XLA Modules:
  0.0 109.4 jit_solution(6239295762410393065)
XLA Ops:
  0.6 0.0 copy-start
  0.6 1.6 %copy-done = f32[512,8,128]{2,1,0:T(8,128)S(1)} copy-done((f32[512,8,128]{2,1,0:T(8,128)S(1)}, f32[512,8,128]{2,1,0:T(8,128)}, u32[]{:S(2)}) %copy-start) | copy-done | bytes 2097176
  2.2 1.6 %gram.1 = (f32[1152,128]{1,0:T(8,128)S(1)}, bf16[512,1024]{1,0:T(8,128)(2,1)S(1)}, bf16[512,1024]{1,0:T(8,128)(2,1)S(1)}) custom-call(f32[512,8,128]{2,1,0:T(8,128)S(1)} %copy-done), custom_call_target="tpu_custom_call" | custom-call | tf_op jit(solution)/shard_map/gram/pallas_call | solution.py:247
  3.9 21.9 %all_to_all.33 = f32[32,9,4,128]{3,2,1,0:T(4,128)S(1)} all-to-all(f32[32,9,4,128]{3,2,1,0:T(4,128)S(1)} %bitcast.9), channel_id=1, replica_groups=mesh['row'=16,'zh'=4,'zl'=4,'core'=2] {'row','core'}, dimensions={0} | all-to-all | bytes 1179648 | tf_op jit(solution)/shard_map/all_to_all | solution.py:235
  25.8 0.0 copy-start.1
  25.8 0.1 reduce_sum.18
  25.9 29.8 %all_to_all.34 = f32[16,9,4,128]{3,2,1,0:T(4,128)S(1)} all-to-all(f32[16,9,4,128]{3,2,1,0:T(4,128)S(1)} %broadcast_in_dim.6), channel_id=1, replica_groups=mesh['row'=16,'zh'=4,'zl'=4,'core'=2] {'zh','zl'}, dimensions={0} | all-to-all | bytes 589824 | tf_op jit(solution)/shard_map/all_to_all | solution.py:235
  55.8 0.1 reduce_sum.19
  55.8 0.1 broadcast_in_dim.7
  55.9 19.7 %all_to_all.35 = f32[32,9,4,128]{3,2,1,0:T(4,128)S(1)} all-to-all(f32[32,9,4,128]{3,2,1,0:T(4,128)S(1)} %broadcast_in_dim.7), channel_id=1, replica_groups=mesh['row'=16,'zh'=4,'zl'=4,'core'=2] {'row','core'}, dimensions={0} | all-to-all | bytes 1179648 | tf_op jit(solution)/shard_map/all_to_all | solution.py:235
  75.6 0.0 copy-done.1
  75.6 14.0 %basis.1 = (f32[256,8,128]{2,1,0:T(8,128)S(1)}, f32[512,256]{1,0:T(8,128)}) custom-call(f32[1152,128]{1,0:T(8,128)S(1)} %bitcast.8, f32[512,256]{1,0:T(8,128)S(1)} %copy-done.1, bf16[512,1024]{1,0:T(8,128)(2,1)S(1)} %get-tuple-element.8.high_ref, bf16[512,1024]{1,0:T(8,128)(2,1)S(1)} %get-tuple-element.9.low_ref), custom_call_target="tpu_custom_call" | custom-call | tf_op jit(solution)/shard_map/basis/pallas_call | solution.py:262
  89.5 18.8 %all_to_all.36 = f32[256,8,128]{2,1,0:T(8,128)S(1)} all-to-all(f32[256,8,128]{2,1,0:T(8,128)S(1)} %get-tuple-element.10), channel_id=1, replica_groups=mesh['row'=16,'zh'=4,'zl'=4,'core'=2] {'row'}, dimensions={0} | all-to-all | bytes 2097152 | tf_op jit(solution)/shard_map/all_to_all | solution.py:278
  108.4 1.1 copy.10
  (1 shorter events, 0.0 us)
Async XLA Ops:
  0.6 1.6 %copy-start = (f32[512,8,128]{2,1,0:T(8,128)S(1)}, f32[512,8,128]{2,1,0:T(8,128)}, u32[]{:S(2)}) copy-start(f32[512,8,128]{2,1,0:T(8,128)} %x_ref.1) | copy-start | bytes 6291460
  25.8 49.8 %copy-start.1 = (f32[512,256]{1,0:T(8,128)S(1)}, f32[512,256]{1,0:T(8,128)}, u32[]{:S(2)}) copy-start(f32[512,256]{1,0:T(8,128)} %start_ref.1) | copy-start | bytes 1572868
